TPU v7x, 768 devices: a whole 4x8x12 slice. The times are simulated.
768 devices in a mesh: wire: 128 (over z_hi, y, x, core), depth: 6 (over z_lo).
Axes of the slice: x: 4, y: 8, z: 12 (z_hi: 2, z_lo: 6; z = z_hi * 6 + z_lo), core: 2. Of those that a mesh axis runs over, the one named last changes fastest.
Arguments:
- density: float32 [768, 64, 1600], P('wire'), as said below
- pattern: int32 [768, 25], P('wire'), may hold values from 0 to 1, as said below
Outputs:
- purified: float32 [768, 64, 1600], P(('wire', 'depth'))
Inputs may be any that keep to these rules, and one draw needn't show every extreme that they name: The pattern is symmetric: pattern[i, d] equals pattern[(i + d - 12) mod 768, 24 - d]; the diagonal block is always present. The density matrix is symmetric and its blocks are zero where the pattern is 0.
All inputs are finite; a program needn't handle non-finite values.
Results may differ from a plain program's by a relative error of at most 0.0001.
Values sent between devices are 32-bit elements; how exact they have to be, the bound alone decides.
A program may use at most 64 MiB of HBM per device.

v0:
```python
import jax
import jax.numpy as jnp
from jax import lax
from jax.sharding import PartitionSpec as P


def shifted(shard, axis, by):
    length = lax.axis_size(axis)
    return lax.ppermute(shard, axis, [(i, (i + by) % length) for i in range(length)])


def neighbours(piece, reach):
    received = {}
    for hop in list(range(1, reach + 1)) + list(range(-reach, 0)):
        received[hop] = shifted(piece, "wire", hop)
    return received


def inner_plan(density, maskband, member, depth, reach):
    rows, orb, cols = density.shape
    width = cols // orb
    half = (width - 1) // 2
    span = (2 * reach + 1) * rows
    picks = span // depth
    outer = span + 2 * half
    share_rows = rows // depth
    zero_index = jnp.zeros((), jnp.int32)
    grouped = density.reshape(share_rows, depth, orb, cols)
    own = lax.dynamic_index_in_dim(grouped, member, 1, keepdims=False)
    received = neighbours(own, reach)
    ordered = (
        [received[h] for h in range(reach, 0, -1)]
        + [own]
        + [received[-h] for h in range(1, reach + 1)]
    )
    far_rows = jnp.concatenate(ordered, axis=0)

    def place_far(line, offset):
        canvas = jnp.zeros((orb, outer * orb), jnp.float32)
        return lax.dynamic_update_slice(canvas, line, (zero_index, offset * orb))

    far_offsets = member + depth * jnp.arange(picks, dtype=jnp.int32)
    right_dense = jax.vmap(place_far)(far_rows, far_offsets).reshape(picks * orb, outer * orb)

    def spread(band):

        def place_near(line, index):
            canvas = jnp.zeros((orb, span * orb), jnp.float32)
            return lax.dynamic_update_slice(
                canvas, line, (zero_index, (reach * rows - half + index) * orb)
            )

        placed = jax.vmap(place_near)(band, jnp.arange(rows, dtype=jnp.int32))
        return placed.reshape(rows * orb, picks, depth, orb)

    def select_share(dense):
        picked = lax.dynamic_index_in_dim(dense, member, 2, keepdims=False)
        return picked.reshape(rows * orb, picks * orb)

    def extract(product):
        lines = product.reshape(rows, orb, outer * orb)

        def cut(line, index):
            return lax.dynamic_slice_in_dim(line, (reach * rows + index) * orb, cols, 1)

        return jax.vmap(cut)(lines, jnp.arange(rows, dtype=jnp.int32))

    def multiply(left_share):
        product = jnp.dot(
            left_share,
            right_dense,
            precision=lax.Precision.HIGHEST,
            preferred_element_type=jnp.float32,
        )
        return extract(product) * maskband

    square_part = multiply(select_share(spread(density)))
    return (square_part, multiply, spread, select_share)


def on_device(density, pattern):
    rows, orb, cols = density.shape
    width = cols // orb
    half = (width - 1) // 2
    depth = lax.axis_size("depth")
    member = lax.axis_index("depth")
    reach = (half + rows - 1) // rows
    share_rows = rows // depth
    maskband = jnp.repeat(pattern.astype(jnp.float32), orb, axis=1)[:, None, :]
    square_part, multiply, spread, select_share = inner_plan(
        density, maskband, member, depth, reach
    )
    square = lax.psum(square_part, "depth")
    cube_part = multiply(select_share(spread(square)))
    extra = 3.0 * lax.dynamic_slice_in_dim(square, member * share_rows, share_rows, 0)
    return lax.psum_scatter(-2.0 * cube_part, "depth", scatter_dimension=0, tiled=True) + extra


def solution(mesh):
    in_specs = (P("wire", None, None), P("wire", None))
    out_specs = P(("wire", "depth"), None, None)
    return jax.shard_map(
        on_device, mesh=mesh, in_specs=in_specs, out_specs=out_specs, check_vma=False
    )
```

profile of v0, /device:TPU:1, one launch (start us, length us, event | category | flops | bytes accessed | tf_op | source)
XLA Modules:
  0.0 518.7 jit_solution(10073019712839865179)
XLA Ops:
  8.3 3.9 collective-permute-start
  12.3 4.0 collective-permute-start.1
  16.3 8.4 %collective-permute-start.2 = (f32[1,64,1600]{2,1,0:T(8,128)}, f32[1,64,1600]{2,1,0:T(8,128)}, u32[]{:S(2)}, u32[]{:S(2)}) collective-permute-start(f32[1,64,1600]{2,1,0:T(8,128)} %constant_dynamic-slice_fusion.5), channel_id=1, source_target_pairs={{0,762},{6,0},{12,6},{18,12},{24,18},{30,24},{36,30},{42,36},{48,4... | collective-permute-start | bytes 1228808 | tf_op jit(solution)/shard_map/ppermute | solution.py:9
  24.6 14.2 %collective-permute-start.3 = (f32[1,64,1600]{2,1,0:T(8,128)}, f32[1,64,1600]{2,1,0:T(8,128)}, u32[]{:S(2)}, u32[]{:S(2)}) collective-permute-start(f32[1,64,1600]{2,1,0:T(8,128)} %constant_dynamic-slice_fusion.5), channel_id=1, source_target_pairs={{0,756},{6,762},{12,0},{18,6},{24,12},{30,18},{36,24},{42,30},{48,... | collective-permute-start | bytes 1228808 | tf_op jit(solution)/shard_map/ppermute | solution.py:9
  39.2 61.9 %while.7 = (s32[]{:T(128)}, f32[6,64,1920]{2,1,0:T(8,128)S(1)}, s32[6,3]{0,1:T(4,128)S(1)}, f32[6,64,1600]{2,1,0:T(8,128)}, s32[]{:T(128)}, /*index=5*/s32[3]{0:T(128)S(1)}, s32[]{:T(128)}) while((s32[]{:T(128)}, f32[6,64,1920]{2,1,0:T(8,128)S(1)}, s32[6,3]{0,1:T(4,128)S(1)}, f32[6,64,1600]{2,1,0:T(8,128)}, s32[]{:T(128)}, ...), condition=%wide.while_cond.2, body=%wide.while_body.2.sunk | while | flops 102419 | bytes 2048171 | solution.py:49
  45.1 4.2 dynamic-update-slice.29
  55.3 4.8 dynamic-update-slice.29
  66.1 4.1 dynamic-update-slice.29
  76.2 4.7 dynamic-update-slice.29
  96.6 4.4 dynamic-update-slice.29
  101.1 4.0 reshape.80
  105.2 6.3 %dynamic-slice_reduce_fusion.1 = f32[384,5,64]{2,1,0:T(8,128)S(1)} fusion(f32[384,5,6,64]{3,2,1,0:T(8,128)} %reshape.80, s32[]{:T(128)S(6)} %select_n.41), kind=kLoop, calls=%fused_computation.16 | loop fusion | bytes 983044 | tf_op jit(solution)/shard_map/jit(dynamic_index_in_dim)/dynamic_slice | solution.py:57
  119.6 52.8 %while.8 = (s32[]{:T(128)}, f32[5,64,3456]{2,1,0:T(8,128)}, s32[5,3]{0,1:T(4,128)S(1)}, f32[5,64,1600]{2,1,0:T(8,128)S(1)}, s32[]{:T(128)}, /*index=5*/s32[3]{0:T(128)S(1)}, s32[]{:T(128)}) while((s32[]{:T(128)}, f32[5,64,3456]{2,1,0:T(8,128)}, s32[5,3]{0,1:T(4,128)S(1)}, f32[5,64,1600]{2,1,0:T(8,128)S(1)}, s32[]{:T(128)}, ...), condition=%wide.while_cond.3, body=%wide.while_body.3.sunk | while | flops 102419 | bytes 2048171 | solution.py:40
  125.7 4.6 dynamic-update-slice.30
  136.3 4.6 dynamic-update-slice.30
  147.0 4.5 dynamic-update-slice.30
  157.5 4.4 dynamic-update-slice.30
  168.0 4.3 dynamic-update-slice.30
  172.4 12.2 %fusion.5 = f32[6,64,3456]{2,1,0:T(8,128)} fusion(f32[6,64,320]{2,1,0:T(8,128)S(1)} %reshape.217, f32[320,3456,1]{1,0,2:T(8,128)} %bitcast.64), kind=kOutput, calls=%fused_computation.39 | convolution fusion | flops 5096079360 | bytes 10223616 | tf_op jit(solution)/shard_map/dot_general | solution.py:69
  184.7 18.8 %while.5 = (s32[]{:T(128)}, f32[6,64,3456]{2,1,0:T(8,128)}, s32[6,3]{0,1:T(4,128)S(1)}, f32[6,64,1600]{2,1,0:T(8,128)S(1)}, s32[]{:T(128)}) while((s32[]{:T(128)}, f32[6,64,3456]{2,1,0:T(8,128)}, s32[6,3]{0,1:T(4,128)S(1)}, f32[6,64,1600]{2,1,0:T(8,128)S(1)}, s32[]{:T(128)}) %tuple.86), condition=%wide.while_cond, body=%wide.while_body.sunk | while | flops 2 | bytes 835701 | solution.py:64
  205.5 130.2 %all-reduce.5.cloned.1.call-done = f32[6,64,1600]{2,1,0:T(8,128)} async-done(((f32[6,64,1600]{2,1,0:T(8,128)}), f32[6,64,1600]{2,1,0:T(8,128)}) %all-reduce.5.cloned.1.call-update) | async-done | bytes 2457616 | tf_op jit(solution)/shard_map/psum | solution.py:93
  335.9 63.2 %while.9 = (s32[]{:T(128)}, f32[6,64,1920]{2,1,0:T(8,128)S(1)}, s32[6,3]{0,1:T(4,128)S(1)}, f32[6,64,1600]{2,1,0:T(8,128)}, s32[]{:T(128)}, /*index=5*/s32[3]{0:T(128)S(1)}, s32[]{:T(128)}) while((s32[]{:T(128)}, f32[6,64,1920]{2,1,0:T(8,128)S(1)}, s32[6,3]{0,1:T(4,128)S(1)}, f32[6,64,1600]{2,1,0:T(8,128)}, s32[]{:T(128)}, ...), condition=%wide.while_cond.4, body=%wide.while_body.4.sunk | while | flops 102419 | bytes 2048171 | solution.py:49
  342.0 4.2 dynamic-update-slice.31
  352.5 4.8 dynamic-update-slice.31
  363.4 4.1 dynamic-update-slice.31
  373.8 4.7 dynamic-update-slice.31
  394.7 4.4 dynamic-update-slice.31
  399.1 4.0 reshape.82
  403.1 6.3 %dynamic-slice_reduce_fusion = f32[384,5,64]{2,1,0:T(8,128)S(1)} fusion(f32[384,5,6,64]{3,2,1,0:T(8,128)} %reshape.82, s32[]{:T(128)S(6)} %select_n.41), kind=kLoop, calls=%fused_computation.15 | loop fusion | bytes 983044 | tf_op jit(solution)/shard_map/jit(dynamic_index_in_dim)/dynamic_slice | solution.py:57
  409.7 12.2 %fusion.6 = f32[6,64,3456]{2,1,0:T(8,128)} fusion(f32[6,64,320]{2,1,0:T(8,128)S(1)} %reshape.218, f32[320,3456,1]{1,0,2:T(8,128)} %bitcast.65), kind=kOutput, calls=%fused_computation.40 | convolution fusion | flops 5096079360 | bytes 10223616 | tf_op jit(solution)/shard_map/dot_general | solution.py:69
  422.0 19.4 %while.6 = (s32[]{:T(128)}, f32[6,64,3456]{2,1,0:T(8,128)}, s32[6,3]{0,1:T(4,128)S(1)}, f32[6,64,1600]{2,1,0:T(8,128)S(1)}, s32[]{:T(128)}) while((s32[]{:T(128)}, f32[6,64,3456]{2,1,0:T(8,128)}, s32[6,3]{0,1:T(4,128)S(1)}, f32[6,64,1600]{2,1,0:T(8,128)S(1)}, s32[]{:T(128)}) %tuple.99), condition=%wide.while_cond.1, body=%wide.while_body.1.sunk | while | flops 2 | bytes 835701 | solution.py:64
  443.1 66.7 %reduce-scatter.2.cloned.1.call-done = f32[1,64,1600]{2,1,0:T(8,128)} async-done(((f32[6,64,1600]{2,1,0:T(8,128)}), f32[1,64,1600]{2,1,0:T(8,128)}) %reduce-scatter.2.cloned.1.call-update) | async-done | bytes 409616 | tf_op jit(solution)/shard_map/reduce_scatter | solution.py:96
  (149 shorter events, 165.3 us)
Async XLA Ops:
  6.5 32.6 %copy-start = (s32[3]{0:T(128)S(1)}, s32[3]{0:T(128)}, u32[]{:S(2)}) copy-start(s32[3]{0:T(128)} %constant.193) | copy-start | bytes 40
  6.5 329.1 %all-reduce.5.cloned.1.call-start = ((), (), s32[]{:S(2)}) async-start(), calls=%async_computation.1 | async-start | bytes 5111808 | tf_op jit(solution)/shard_map/psum | solution.py:93
  8.3 103.6 %collective-permute-start = (f32[1,64,1600]{2,1,0:T(8,128)}, f32[1,64,1600]{2,1,0:T(8,128)}, u32[]{:S(2)}, u32[]{:S(2)}) collective-permute-start(f32[1,64,1600]{2,1,0:T(8,128)} %constant_dynamic-slice_fusion.5), channel_id=1, source_target_pairs={{0,12},{6,18},{12,24},{18,30},{24,36},{30,42},{36,48},{42,54},{48,... | collective-permute-start | bytes 1228808 | tf_op jit(solution)/shard_map/ppermute | solution.py:9
  12.3 100.7 %collective-permute-start.1 = (f32[1,64,1600]{2,1,0:T(8,128)}, f32[1,64,1600]{2,1,0:T(8,128)}, u32[]{:S(2)}, u32[]{:S(2)}) collective-permute-start(f32[1,64,1600]{2,1,0:T(8,128)} %constant_dynamic-slice_fusion.5), channel_id=1, source_target_pairs={{0,6},{6,12},{12,18},{18,24},{24,30},{30,36},{36,42},{42,48},{48,5... | collective-permute-start | bytes 1228808 | tf_op jit(solution)/shard_map/ppermute | solution.py:9
  16.3 98.8 %collective-permute-start.2 = (f32[1,64,1600]{2,1,0:T(8,128)}, f32[1,64,1600]{2,1,0:T(8,128)}, u32[]{:S(2)}, u32[]{:S(2)}) collective-permute-start(f32[1,64,1600]{2,1,0:T(8,128)} %constant_dynamic-slice_fusion.5), channel_id=1, source_target_pairs={{0,762},{6,0},{12,6},{18,12},{24,18},{30,24},{36,30},{42,36},{48,4... | collective-permute-start | bytes 1228808 | tf_op jit(solution)/shard_map/ppermute | solution.py:9
  24.6 91.5 %collective-permute-start.3 = (f32[1,64,1600]{2,1,0:T(8,128)}, f32[1,64,1600]{2,1,0:T(8,128)}, u32[]{:S(2)}, u32[]{:S(2)}) collective-permute-start(f32[1,64,1600]{2,1,0:T(8,128)} %constant_dynamic-slice_fusion.5), channel_id=1, source_target_pairs={{0,756},{6,762},{12,0},{18,6},{24,12},{30,18},{36,24},{42,30},{48,... | collective-permute-start | bytes 1228808 | tf_op jit(solution)/shard_map/ppermute | solution.py:9
  105.1 6.6 %copy-start.2 = (s32[6,25]{1,0:T(8,128)S(1)}, s32[6,25]{1,0:T(8,128)}, u32[]{:S(2)}) copy-start(s32[6,25]{1,0:T(8,128)} %param.3) | copy-start | bytes 1804
  116.2 3.4 copy-start.1
  205.2 304.7 %reduce-scatter.2.cloned.1.call-start = ((), (), s32[]{:S(2)}) async-start(), calls=%async_computation.2 | async-start | bytes 2981888 | tf_op jit(solution)/shard_map/reduce_scatter | solution.py:96
Sparse Core Ops, SparseCore 0:
  205.4 130.2 all-reduce.4
  443.3 66.5 reduce-scatter.1
where the time goes:
time: 522 us; the launch traced here: 519 us
  waiting for transfers between devices  197 us (38%)
  local copies, waits for them, and re-layouts  155 us (30%)
  other arithmetic  97.8 us (19%)
  starting transfers between devices  30.7 us (6%)
  matrix products  24.3 us (5%)
  between operations  13.6 us (3%)
    psum x1, waiting for transfers between devices, on_device(): square = lax.psum(square_part, 'depth')  130 us
    scatter x34, other arithmetic  92.2 us
    scatter x51, local copies, waits for them, and re-layouts  85.2 us
    reduce_scatter x1, waiting for transfers between devices, on_device(): lax.psum_scatter(-2.0 * cube_part, 'depth', scatter_dimension=0, tiled=True)  66.7 us
    gather x36, local copies, waits for them, and re-layouts  38 us
    ppermute x4, starting transfers between devices, shifted(): lax.ppermute(shard, axis, [(i, (i + by) % length) for i in range(length)])  30.4 us
    dot_general x2, matrix products, multiply(): jnp.dot(left_share, right_dense, precision=lax.Precision.HIGHEST, preferr...  24.3 us
    dynamic_slice x2, local copies, waits for them, and re-layouts, select_share(): picked = lax.dynamic_index_in_dim(dense, member, 2, keepdims=False)  12.5 us
  transfers between devices with their start and end apart: 6, of which 2 were waited for; matrix products, arithmetic and copies ran while one was open for 15% of the time, Pallas kernels for 0%

commit v1 on v0

v1 whole, which is shorter than its diff:
```python
import jax
import jax.numpy as jnp
from jax import lax
from jax.experimental import pallas as pl
from jax.experimental.pallas import tpu as pltpu
from jax.sharding import PartitionSpec as P

MESH = pl.DeviceIdType.MESH
ORB = 64
ROWS = 6
CHIP = 2 * ROWS
FRAME = 3 * CHIP * ORB
SIDE = CHIP * ORB
HALFSIDE = ROWS * ORB
BAND = 25 * ORB
BANDPAD = 26 * ORB
TILE = 256
DIAG = 12 * ORB
F32 = jnp.float32
BF16 = jnp.bfloat16


def member():
    return lax.axis_index("depth")


def lanes(blocks):
    return (blocks + 1) // 2 * 2 * ORB


def split(x):
    high = x.astype(BF16)
    low = (x - high.astype(F32)).astype(BF16)
    return high, low


def symmetrized(tile):
    size = tile.shape[0]
    row = lax.broadcasted_iota(jnp.int32, (size, size), 0) >> 6
    col = lax.broadcasted_iota(jnp.int32, (size, size), 1) >> 6
    tile = tile.astype(F32)
    return jnp.where(row <= col, tile, tile.T).astype(BF16)


def kernel(
    density, pattern, out,
    rows, big, small, wc_hi, wc_lo, big_hi, big_lo, small_hi, small_lo,
    left, middle, square, cube, maskrow,
    own_sem, pair_send, pair_recv, up_send, down_send, big_recv, fwd_send, fwd_recv,
):
    wire = lax.axis_index("wire")
    length = lax.axis_size("wire")
    m = member()
    h = lax.rem(wire, 2)
    other = wire + 1 - 2 * h
    up = lax.rem(wire - h + 2, length)
    down = lax.rem(wire - h - 1 + length, length)
    source = lax.rem(wire - h + 4 * h - 2 + length, length)

    own = pltpu.make_async_copy(density, rows.at[pl.ds(ROWS * h, ROWS)], own_sem)
    own.start()

    barrier = pltpu.get_barrier_semaphore()
    for sender in (other, source, source + 1):
        pl.semaphore_signal(barrier, inc=1, device_id={"wire": sender}, device_id_type=MESH)
    pl.semaphore_wait(barrier, 3)

    pair = pltpu.make_async_remote_copy(
        src_ref=density, dst_ref=rows.at[pl.ds(ROWS * h, ROWS)],
        send_sem=pair_send, recv_sem=pair_recv,
        device_id={"wire": other}, device_id_type=MESH,
    )

    def outgoing(core):
        copies = []
        for s in range(ROWS):
            t = ROWS * core + s
            width = lanes(CHIP - t)
            for target, sem in ((up, up_send), (down, down_send)):
                copies.append(pltpu.make_async_remote_copy(
                    src_ref=density.at[s, :, pl.ds(DIAG, width)],
                    dst_ref=big.at[t, :, pl.ds(0, width)],
                    send_sem=sem.at[s], recv_sem=big_recv.at[t],
                    device_id={"wire": target}, device_id_type=MESH,
                ))
        return copies

    def arriving(t):
        width = lanes(CHIP - t)
        return pltpu.make_async_remote_copy(
            src_ref=density.at[t % ROWS, :, pl.ds(DIAG, width)],
            dst_ref=big.at[t, :, pl.ds(0, width)],
            send_sem=up_send.at[t % ROWS], recv_sem=big_recv.at[t],
            device_id={"wire": up}, device_id_type=MESH,
        )

    def forward(s):
        width = lanes(ROWS - s)
        return pltpu.make_async_remote_copy(
            src_ref=big.at[ROWS * (1 - h) + s, :, pl.ds(0, width)],
            dst_ref=small.at[s, :, pl.ds(0, width)],
            send_sem=fwd_send.at[s], recv_sem=fwd_recv.at[s],
            device_id={"wire": other}, device_id_type=MESH,
        )

    for core in range(2):
        @pl.when(h == core)
        def _(core=core):
            for copy in outgoing(core):
                copy.start()
    pair.start()

    wc_hi[...] = jnp.zeros_like(wc_hi)
    wc_lo[...] = jnp.zeros_like(wc_lo)
    place = ROWS * h + m

    def band_row(index):
        x = rows[index]
        return jnp.concatenate([x, jnp.zeros((ORB, BANDPAD - BAND), F32)], axis=1)

    def build_centre(half):
        for s in range(ROWS):
            x = band_row(ROWS * half + s)
            if s % 2:
                x = pltpu.roll(x, ORB, 1)
            high, low = split(x)
            down_by = pl.ds(pl.multiple_of(half * HALFSIDE + s * ORB, ORB), ORB)
            along = pl.ds(pl.multiple_of(half * HALFSIDE + (s - s % 2) * ORB, 128), BANDPAD)
            wc_hi[down_by, along] = high
            wc_lo[down_by, along] = low

    own.wait()
    build_centre(h)

    def framed(x):
        wide = jnp.concatenate([x, jnp.zeros((x.shape[0], FRAME - BANDPAD), F32)], axis=1)
        return pltpu.roll(wide, place * ORB, 1)

    def stack(ref, x, along):
        high, low = split(x)
        ref[0:ORB, along] = high
        ref[ORB:2 * ORB, along] = low

    stack(left, framed(band_row(place)), slice(0, FRAME))

    block = lax.broadcasted_iota(jnp.int32, (8, BANDPAD), 1) >> 6
    bits = jnp.zeros((8, BANDPAD), F32)
    for d in range(25):
        bits = jnp.where(block == d, pattern[m, d].astype(F32), bits)
    maskrow[...] = framed(bits)

    def product(ref, along, high, low, across):
        dims = (((1,), (1 if across else 0,)), ((), ()))
        first = lax.dot_general(ref[:, along], high, dims, preferred_element_type=F32)
        second = lax.dot_general(ref[0:ORB, along], low, dims, preferred_element_type=F32)
        return first[0:ORB] + first[ORB:2 * ORB] + second

    def centre(ref, acc):
        for b in range(9):
            a0, a1 = max(0, b - 6), min(3, b + 1)
            down_by = slice(a0 * TILE, a1 * TILE)
            along = slice(b * TILE, (b + 1) * TILE)
            acc[:, along] = product(
                ref, slice(SIDE + a0 * TILE, SIDE + a1 * TILE),
                wc_hi[down_by, along], wc_lo[down_by, along], False,
            )

    def sides(ref, acc):
        for a in range(3):
            down_by = slice(a * TILE, (a + 1) * TILE)
            lo = slice(a * TILE, SIDE)
            hi = slice(2 * SIDE, 2 * SIDE + (a + 1) * TILE)
            acc[:, SIDE + a * TILE:SIDE + (a + 1) * TILE] += (
                product(ref, lo, wc_hi[down_by, lo], wc_lo[down_by, lo], True)
                + product(ref, hi, wc_hi[down_by, hi], wc_lo[down_by, hi], True)
            )

    big_at = h * (2 * SIDE)
    small_at = 2 * SIDE - h * (2 * SIDE - HALFSIDE)

    def corners(ref, acc):
        for b in range(3):
            here = pl.ds(pl.multiple_of(big_at + b * TILE, 128), TILE)
            upto = (b + 1) * TILE
            total = product(
                ref, pl.ds(pl.multiple_of(big_at, 128), upto),
                big_hi[0:upto, b * TILE:upto], big_lo[0:upto, b * TILE:upto], False,
            )
            if b < 2:
                total += product(
                    ref, pl.ds(pl.multiple_of(big_at + upto, 128), SIDE - upto),
                    big_hi[b * TILE:upto, upto:SIDE], big_lo[b * TILE:upto, upto:SIDE], True,
                )
            acc[:, here] += total
        here = pl.ds(pl.multiple_of(small_at, 128), HALFSIDE)
        acc[:, here] += product(ref, here, small_hi[...], small_lo[...], False)

    pair.wait_recv()
    build_centre(1 - h)

    centre(left, square)
    sides(left, square)
    mid = slice(SIDE, 2 * SIDE)
    masked = square[:, mid] * maskrow[0:1, mid]
    square[:, mid] = masked
    stack(middle, masked, mid)
    centre(middle, cube)

    for core in range(2):
        @pl.when(h == core)
        def _(core=core):
            for s in range(ROWS):
                arriving(ROWS * (1 - core) + s).wait_recv()
    for s in range(ROWS):
        forward(s).start()
    for core in range(2):
        @pl.when(h == core)
        def _(core=core):
            for s in range(ROWS):
                arriving(ROWS * core + s).wait_recv()

    def build_triangle(source_ref, high_ref, low_ref, count):
        for t in range(count):
            x = source_ref[t, :, 0:lanes(count - t)]
            if t % 2:
                x = pltpu.roll(x, ORB, 1)
                lane = lax.broadcasted_iota(jnp.int32, x.shape, 1)
                x = jnp.where(lane < ORB, 0.0, x)
            high, low = split(x)
            along = slice((t - t % 2) * ORB, count * ORB)
            high_ref[t * ORB:(t + 1) * ORB, along] = high
            low_ref[t * ORB:(t + 1) * ORB, along] = low

    build_triangle(big, big_hi, big_lo, CHIP)
    for ref in (big_hi, big_lo):
        for a in range(3):
            tile = slice(a * TILE, (a + 1) * TILE)
            ref[tile, tile] = symmetrized(ref[tile, tile])
    for s in range(ROWS):
        forward(s).wait_recv()
    build_triangle(small, small_hi, small_lo, ROWS)
    for ref in (small_hi, small_lo):
        ref[...] = symmetrized(ref[...])

    corners(left, square)
    for along in (slice(0, SIDE), slice(2 * SIDE, FRAME)):
        masked = square[:, along] * maskrow[0:1, along]
        square[:, along] = masked
        stack(middle, masked, along)
    sides(middle, cube)
    corners(middle, cube)

    result = 3.0 * square[...] - 2.0 * (cube[...] * maskrow[0:1, :])
    out[0] = pltpu.roll(result, FRAME - place * ORB, 1)[:, 0:BAND]

    for core in range(2):
        @pl.when(h == core)
        def _(core=core):
            for copy in outgoing(core):
                copy.wait_send()
    pair.wait_send()
    for s in range(ROWS):
        forward(s).wait_send()


def on_device(density, pattern):
    dma = pltpu.SemaphoreType.DMA
    return pl.pallas_call(
        kernel,
        out_shape=jax.ShapeDtypeStruct((1, ORB, BAND), F32),
        in_specs=[pl.BlockSpec(memory_space=pl.ANY), pl.BlockSpec(memory_space=pltpu.SMEM)],
        out_specs=pl.BlockSpec(memory_space=pltpu.VMEM),
        scratch_shapes=[
            pltpu.VMEM((CHIP, ORB, BAND), F32),
            pltpu.VMEM((CHIP, ORB, SIDE), F32),
            pltpu.VMEM((ROWS, ORB, HALFSIDE), F32),
            pltpu.VMEM((SIDE, FRAME), BF16),
            pltpu.VMEM((SIDE, FRAME), BF16),
            pltpu.VMEM((SIDE, SIDE), BF16),
            pltpu.VMEM((SIDE, SIDE), BF16),
            pltpu.VMEM((HALFSIDE, HALFSIDE), BF16),
            pltpu.VMEM((HALFSIDE, HALFSIDE), BF16),
            pltpu.VMEM((2 * ORB, FRAME), BF16),
            pltpu.VMEM((2 * ORB, FRAME), BF16),
            pltpu.VMEM((ORB, FRAME), F32),
            pltpu.VMEM((ORB, FRAME), F32),
            pltpu.VMEM((8, FRAME), F32),
            dma, dma, dma, dma((ROWS,)), dma((ROWS,)), dma((CHIP,)), dma((ROWS,)), dma((ROWS,)),
        ],
        compiler_params=pltpu.CompilerParams(
            collective_id=0, has_side_effects=True, vmem_limit_bytes=48 * 1024 * 1024
        ),
    )(density, pattern)


def solution(mesh):
    in_specs = (P("wire", None, None), P("wire", None))
    out_specs = P(("wire", "depth"), None, None)
    return jax.shard_map(
        on_device, mesh=mesh, in_specs=in_specs, out_specs=out_specs, check_vma=False
    )
```

time: 522 us -> 69.6 us (0.13)
  the two profiles are of different devices: /device:TPU:1 before, /device:TPU:192 now
where the time goes in v1:
time: 69.6 us; the launch traced here: 69.4 us
  Pallas kernels  66.2 us (95%)
  local copies, waits for them, and re-layouts  3.17 us (5%)
    pallas_call x1, Pallas kernels, on_device(): pl.pallas_call(kernel, out_shape=jax.ShapeDtypeStruct((1, ORB, BAND), F32...  66.2 us
    unnamed x5, local copies, waits for them, and re-layouts  3.17 us

profile of v1, /device:TPU:192, one launch (start us, length us, event | category | flops | bytes accessed | tf_op | source)
XLA Modules:
  0.0 69.4 jit_solution(7327527766068945714)
XLA Ops:
  0.0 0.0 copy-start
  0.0 1.7 %copy-done = f32[6,64,1600]{2,1,0:T(8,128)S(1)} copy-done((f32[6,64,1600]{2,1,0:T(8,128)S(1)}, f32[6,64,1600]{2,1,0:T(8,128)}, u32[]{:S(2)}) %copy-start) | copy-done | bytes 2457624
  1.7 0.0 copy-start.1
  1.7 0.7 copy-done.1
  2.4 66.2 %shard_map.28 = f32[1,64,1600]{2,1,0:T(8,128)S(1)} custom-call(f32[6,64,1600]{2,1,0:T(8,128)S(1)} %copy-done, s32[6,25]{1,0:T(8,128)S(1)} %copy-done.1), custom_call_target="tpu_custom_call" | custom-call | tf_op jit(solution)/shard_map/pallas_call | solution.py:268
  68.6 0.8 %copy.4 = f32[1,64,1600]{2,1,0:T(8,128)} copy(f32[1,64,1600]{2,1,0:T(8,128)S(1)} %shard_map.28) | data formatting | bytes 819200
Async XLA Ops:
  0.0 1.7 %copy-start = (f32[6,64,1600]{2,1,0:T(8,128)S(1)}, f32[6,64,1600]{2,1,0:T(8,128)}, u32[]{:S(2)}) copy-start(f32[6,64,1600]{2,1,0:T(8,128)} %density.1) | copy-start | bytes 7372804
  1.7 0.7 copy-start.1

commit v2 on v1

--- a/solution.py
+++ b/solution.py
@@ -20,8 +20,30 @@
 BF16 = jnp.bfloat16
 
 
-def member():
-    return lax.axis_index("depth")
+FIRST = (8, 10, 5, 2, 1, 0)
+SECOND = (6, 7, 9, 11, 4, 3)
+LEFT_ORDER = (
+    (8, 10, 5, 2, 1, 6, 7, 9, 11, 4, 3, 0),
+    (8, 10, 5, 6, 7, 9, 11, 2, 4, 1, 3),
+    (6, 7, 9, 11, 8, 10, 5, 4, 3, 2),
+    (6, 7, 9, 11, 4, 3, 8, 10, 5),
+    (6, 7, 9, 11, 4, 8, 10, 5),
+    (6, 7, 9, 11, 8, 10, 5),
+)
+LEFT_NEXT = (
+    {1: FIRST},
+    {2: FIRST, 0: SECOND},
+    {3: FIRST + SECOND, 1: SECOND},
+    {4: FIRST + SECOND},
+    {5: FIRST + SECOND},
+    {},
+)
+RIGHT_REACH = (9, 9, 9, 10, 11, 12)
+RIGHT_NEXT = ((1,), (2,), (), (), (3,), (4,))
+NEXT = (LEFT_NEXT, RIGHT_NEXT)
+ENTRY = ({5: 0, 0: 2}, {5: 0, 0: 5})
+EARLY_GIVER = (((1, 0), (1, 2), (2, 3), (3, 4), (4, 5)), ((0, 1), (1, 2)))
+NEAR_FIRST = (6, 0, 7, 8, 1, 9, 10, 11, 2, 3, 4, 5)
 
 
 def lanes(blocks):
@@ -43,14 +65,17 @@
 
 
 def kernel(
-    density, pattern, out,
-    rows, big, small, wc_hi, wc_lo, big_hi, big_lo, small_hi, small_lo,
+    density, pattern_in, out,
+    pattern, rows, big, small, wc_hi, wc_lo, big_hi, big_lo, small_hi, small_lo,
     left, middle, square, cube, maskrow,
-    own_sem, pair_send, pair_recv, up_send, down_send, big_recv, fwd_send, fwd_recv,
+    pattern_sem, own_sem, pair_send, pair_recv, up_send, down_send, big_recv, fwd_send, fwd_recv, relay_a, relay_b, ready,
 ):
     wire = lax.axis_index("wire")
     length = lax.axis_size("wire")
-    m = member()
+    me = lax.axis_index("depth")
+    m = me
+    half = length // 4
+    spot = lax.rem(wire // 2, half)
     h = lax.rem(wire, 2)
     other = wire + 1 - 2 * h
     up = lax.rem(wire - h + 2, length)
@@ -59,55 +84,216 @@
 
     own = pltpu.make_async_copy(density, rows.at[pl.ds(ROWS * h, ROWS)], own_sem)
     own.start()
-
+    bits_in = pltpu.make_async_copy(pattern_in, pattern, pattern_sem)
+    bits_in.start()
+
+    first = spot == 0
+    last = spot == half - 1
+    seam_left = jnp.logical_and(h == 0, first)
+    seam_right = jnp.logical_and(h == 1, last)
+    seam = jnp.logical_or(seam_left, seam_right)
+    ends = jnp.logical_or(m == 0, m == 5)
+    late = 2 * wire >= length
+    early = jnp.logical_not(late)
     barrier = pltpu.get_barrier_semaphore()
-    for sender in (other, source, source + 1):
-        pl.semaphore_signal(barrier, inc=1, device_id={"wire": sender}, device_id_type=MESH)
-    pl.semaphore_wait(barrier, 3)
+
+    def greet(w, d):
+        pl.semaphore_signal(barrier, inc=1, device_id={"wire": w, "depth": d}, device_id_type=MESH)
+
+    def when(cond, *more):
+        for c in more:
+            if c is not True:
+                cond = jnp.logical_and(cond, c)
+        return pl.when(cond)
+
+    @pl.when(seam)
+    def _():
+        big[...] = jnp.zeros_like(big)
+
+    greet(other, me)
+    expected = jnp.int32(1)
+
+    def counted(cond, n):
+        return jnp.where(cond, n, 0)
+
+    @pl.when(jnp.logical_not(seam))
+    def _():
+        greet(source, me)
+        greet(source + 1, me)
+
+    for end, target in ((first, down), (last, up)):
+        expected += counted(jnp.logical_not(end), 1)
+        expected += counted(jnp.logical_and(end, jnp.logical_and(ends, late)), 1)
+    for side, (end, target) in enumerate(((last, up), (first, down))):
+        for d, entry in ENTRY[side].items():
+            @when(end, early, m == d)
+            def _(target=target, entry=entry):
+                greet(target, entry)
+
+    for kind, here in enumerate((seam_left, seam_right)):
+        for d, entry in ENTRY[kind].items():
+            @when(here, early, m == entry)
+            def _(d=d):
+                greet(source, d)
+                greet(source + 1, d)
+            expected += counted(jnp.logical_and(jnp.logical_and(here, late), m == entry), 2)
+        for giver in range(ROWS):
+            for taker in NEXT[kind][giver]:
+                asks = (giver, taker) in EARLY_GIVER[kind]
+                @when(here, m == (giver if asks else taker))
+                def _(peer=taker if asks else giver):
+                    greet(wire, peer)
+                expected += counted(
+                    jnp.logical_and(here, m == (taker if asks else giver)), 1
+                )
+    pl.semaphore_wait(barrier, expected)
+
+    def is_ready(w, d, slot):
+        pl.semaphore_signal(
+            ready.at[slot], inc=1, device_id={"wire": w, "depth": d}, device_id_type=MESH
+        )
+
+    for kind, here in enumerate((seam_left, seam_right)):
+        for d, entry in ENTRY[kind].items():
+            @when(here, late, m == entry)
+            def _(d=d, kind=kind):
+                is_ready(source, d, kind)
+                is_ready(source + 1, d, kind)
+        for giver in range(ROWS):
+            for n, taker in enumerate(NEXT[kind][giver]):
+                if (giver, taker) in EARLY_GIVER[kind]:
+                    @when(here, m == taker)
+                    def _(giver=giver, n=n):
+                        is_ready(wire, giver, 2 + n)
+
+    def row_copy(s, t, width, target, depth, sem):
+        return pltpu.make_async_remote_copy(
+            src_ref=density.at[s, :, pl.ds(DIAG, width)],
+            dst_ref=big.at[t, :, pl.ds(0, width)],
+            send_sem=sem.at[s], recv_sem=big_recv.at[t],
+            device_id={"wire": target, "depth": depth}, device_id_type=MESH,
+        )
+
+    def send(act, core, order, target, depth, sem, reach):
+        for t in order:
+            if t // ROWS == core and t < reach:
+                act(row_copy(t % ROWS, t, lanes(reach - t), target, depth, sem))
+
+    def outgoing(act):
+        for core in range(2):
+            @when(h == core, jnp.logical_not(last))
+            def _(core=core):
+                send(act, core, NEAR_FIRST, up, me, up_send, CHIP)
+
+            @when(h == core, jnp.logical_not(first))
+            def _(core=core):
+                send(act, core, NEAR_FIRST, down, me, down_send, CHIP)
+
+    def crossing(act, whose, wait):
+        for core in range(2):
+            for d, entry in ENTRY[0].items():
+                @when(h == core, whose, last, m == d)
+                def _(core=core, d=d, entry=entry):
+                    if wait:
+                        pl.semaphore_wait(ready.at[0], 1)
+                    send(act, core, FIRST if d else SECOND, up, entry, up_send, CHIP)
+
+            for d, entry in ENTRY[1].items():
+                @when(h == core, whose, first, m == d)
+                def _(core=core, d=d, entry=entry):
+                    if wait:
+                        pl.semaphore_wait(ready.at[1], 1)
+                    reach = RIGHT_REACH[2] if d else CHIP
+                    send(act, core, NEAR_FIRST, down, entry, down_send, reach)
+
+    def arriving(t, width):
+        return row_copy(t % ROWS, t, width, up, me, up_send)
+
+    def relay(t, width, depth, sem):
+        return pltpu.make_async_remote_copy(
+            src_ref=big.at[t, :, pl.ds(0, width)],
+            dst_ref=big.at[t, :, pl.ds(0, width)],
+            send_sem=sem.at[t], recv_sem=big_recv.at[t],
+            device_id={"wire": wire, "depth": depth}, device_id_type=MESH,
+        )
+
+    def forward(s, core):
+        width = lanes(ROWS - s)
+        return pltpu.make_async_remote_copy(
+            src_ref=big.at[ROWS * (1 - core) + s, :, pl.ds(0, width)],
+            dst_ref=small.at[s, :, pl.ds(0, width)],
+            send_sem=fwd_send.at[s], recv_sem=fwd_recv.at[s],
+            device_id={"wire": other}, device_id_type=MESH,
+        )
+
+    def hand_on(t, core):
+        if t // ROWS == 1 - core:
+            forward(t % ROWS, core).start()
+
+    def relays(kind, i):
+        if kind == 0:
+            for n, (target, which) in enumerate(LEFT_NEXT[i].items()):
+                sem = (relay_a, relay_b)[n]
+                for t in LEFT_ORDER[i]:
+                    if t in which and t in LEFT_ORDER[target]:
+                        yield t, relay(t, lanes(CHIP - t), target, sem)
+        for target in RIGHT_NEXT[i] if kind else ():
+            for t in NEAR_FIRST:
+                if t < RIGHT_REACH[target]:
+                    yield t, relay(t, lanes(RIGHT_REACH[target] - t), target, relay_a)
+
+    def collect():
+        for core in range(2):
+            @when(h == core, jnp.logical_not(seam))
+            def _(core=core):
+                for t in NEAR_FIRST:
+                    if t // ROWS == 1 - core:
+                        arriving(t, lanes(CHIP - t)).wait_recv()
+                        hand_on(t, core)
+                for t in NEAR_FIRST:
+                    if t // ROWS == core:
+                        arriving(t, lanes(CHIP - t)).wait_recv()
+        for i in range(ROWS):
+            for kind, here in enumerate((seam_left, seam_right)):
+                @when(here, m == i)
+                def _(i=i, kind=kind):
+                    order = NEAR_FIRST if kind else LEFT_ORDER[i]
+                    reach = RIGHT_REACH[i] if kind else CHIP
+                    onward = list(relays(kind, i))
+                    for n, taker in enumerate(NEXT[kind][i]):
+                        if (i, taker) in EARLY_GIVER[kind]:
+                            pl.semaphore_wait(ready.at[2 + n], 1)
+                    for t in order:
+                        if t < reach:
+                            arriving(t, lanes(reach - t)).wait_recv()
+                            for u, copy in onward:
+                                if u == t:
+                                    copy.start()
+                            hand_on(t, kind)
+
+    def drain():
+        outgoing(lambda copy: copy.wait_send())
+        crossing(lambda copy: copy.wait_send(), True, False)
+        pair.wait_send()
+        for core in range(2):
+            @pl.when(h == core)
+            def _(core=core):
+                for s in range(ROWS):
+                    forward(s, core).wait_send()
+        for i in range(ROWS):
+            for kind, here in enumerate((seam_left, seam_right)):
+                @when(here, m == i)
+                def _(i=i, kind=kind):
+                    for _, copy in relays(kind, i):
+                        copy.wait_send()
 
     pair = pltpu.make_async_remote_copy(
         src_ref=density, dst_ref=rows.at[pl.ds(ROWS * h, ROWS)],
         send_sem=pair_send, recv_sem=pair_recv,
         device_id={"wire": other}, device_id_type=MESH,
     )
-
-    def outgoing(core):
-        copies = []
-        for s in range(ROWS):
-            t = ROWS * core + s
-            width = lanes(CHIP - t)
-            for target, sem in ((up, up_send), (down, down_send)):
-                copies.append(pltpu.make_async_remote_copy(
-                    src_ref=density.at[s, :, pl.ds(DIAG, width)],
-                    dst_ref=big.at[t, :, pl.ds(0, width)],
-                    send_sem=sem.at[s], recv_sem=big_recv.at[t],
-                    device_id={"wire": target}, device_id_type=MESH,
-                ))
-        return copies
-
-    def arriving(t):
-        width = lanes(CHIP - t)
-        return pltpu.make_async_remote_copy(
-            src_ref=density.at[t % ROWS, :, pl.ds(DIAG, width)],
-            dst_ref=big.at[t, :, pl.ds(0, width)],
-            send_sem=up_send.at[t % ROWS], recv_sem=big_recv.at[t],
-            device_id={"wire": up}, device_id_type=MESH,
-        )
-
-    def forward(s):
-        width = lanes(ROWS - s)
-        return pltpu.make_async_remote_copy(
-            src_ref=big.at[ROWS * (1 - h) + s, :, pl.ds(0, width)],
-            dst_ref=small.at[s, :, pl.ds(0, width)],
-            send_sem=fwd_send.at[s], recv_sem=fwd_recv.at[s],
-            device_id={"wire": other}, device_id_type=MESH,
-        )
-
-    for core in range(2):
-        @pl.when(h == core)
-        def _(core=core):
-            for copy in outgoing(core):
-                copy.start()
+    crossing(lambda copy: copy.start(), late, False)
+    outgoing(lambda copy: copy.start())
     pair.start()
 
     wc_hi[...] = jnp.zeros_like(wc_hi)
@@ -118,14 +304,14 @@
         x = rows[index]
         return jnp.concatenate([x, jnp.zeros((ORB, BANDPAD - BAND), F32)], axis=1)
 
-    def build_centre(half):
+    def build_centre(part):
         for s in range(ROWS):
-            x = band_row(ROWS * half + s)
+            x = band_row(ROWS * part + s)
             if s % 2:
                 x = pltpu.roll(x, ORB, 1)
             high, low = split(x)
-            down_by = pl.ds(pl.multiple_of(half * HALFSIDE + s * ORB, ORB), ORB)
-            along = pl.ds(pl.multiple_of(half * HALFSIDE + (s - s % 2) * ORB, 128), BANDPAD)
+            down_by = pl.ds(pl.multiple_of(part * HALFSIDE + s * ORB, ORB), ORB)
+            along = pl.ds(pl.multiple_of(part * HALFSIDE + (s - s % 2) * ORB, 128), BANDPAD)
             wc_hi[down_by, along] = high
             wc_lo[down_by, along] = low
 
@@ -143,6 +329,7 @@
 
     stack(left, framed(band_row(place)), slice(0, FRAME))
 
+    bits_in.wait()
     block = lax.broadcasted_iota(jnp.int32, (8, BANDPAD), 1) >> 6
     bits = jnp.zeros((8, BANDPAD), F32)
     for d in range(25):
@@ -206,18 +393,8 @@
     stack(middle, masked, mid)
     centre(middle, cube)
 
-    for core in range(2):
-        @pl.when(h == core)
-        def _(core=core):
-            for s in range(ROWS):
-                arriving(ROWS * (1 - core) + s).wait_recv()
-    for s in range(ROWS):
-        forward(s).start()
-    for core in range(2):
-        @pl.when(h == core)
-        def _(core=core):
-            for s in range(ROWS):
-                arriving(ROWS * core + s).wait_recv()
+    crossing(lambda copy: copy.start(), early, True)
+    collect()
 
     def build_triangle(source_ref, high_ref, low_ref, count):
         for t in range(count):
@@ -237,7 +414,7 @@
             tile = slice(a * TILE, (a + 1) * TILE)
             ref[tile, tile] = symmetrized(ref[tile, tile])
     for s in range(ROWS):
-        forward(s).wait_recv()
+        forward(s, 0).wait_recv()
     build_triangle(small, small_hi, small_lo, ROWS)
     for ref in (small_hi, small_lo):
         ref[...] = symmetrized(ref[...])
@@ -253,14 +430,7 @@
     result = 3.0 * square[...] - 2.0 * (cube[...] * maskrow[0:1, :])
     out[0] = pltpu.roll(result, FRAME - place * ORB, 1)[:, 0:BAND]
 
-    for core in range(2):
-        @pl.when(h == core)
-        def _(core=core):
-            for copy in outgoing(core):
-                copy.wait_send()
-    pair.wait_send()
-    for s in range(ROWS):
-        forward(s).wait_send()
+    drain()
 
 
 def on_device(density, pattern):
@@ -268,9 +438,10 @@
     return pl.pallas_call(
         kernel,
         out_shape=jax.ShapeDtypeStruct((1, ORB, BAND), F32),
-        in_specs=[pl.BlockSpec(memory_space=pl.ANY), pl.BlockSpec(memory_space=pltpu.SMEM)],
+        in_specs=[pl.BlockSpec(memory_space=pltpu.HBM)] * 2,
         out_specs=pl.BlockSpec(memory_space=pltpu.VMEM),
         scratch_shapes=[
+            pltpu.SMEM((ROWS, 25), jnp.int32),
             pltpu.VMEM((CHIP, ORB, BAND), F32),
             pltpu.VMEM((CHIP, ORB, SIDE), F32),
             pltpu.VMEM((ROWS, ORB, HALFSIDE), F32),
@@ -285,10 +456,11 @@
             pltpu.VMEM((ORB, FRAME), F32),
             pltpu.VMEM((ORB, FRAME), F32),
             pltpu.VMEM((8, FRAME), F32),
-            dma, dma, dma, dma((ROWS,)), dma((ROWS,)), dma((CHIP,)), dma((ROWS,)), dma((ROWS,)),
+            dma, dma, dma, dma, dma((ROWS,)), dma((ROWS,)), dma((CHIP,)), dma((ROWS,)), dma((ROWS,)),
+            dma((CHIP,)), dma((CHIP,)), pltpu.SemaphoreType.REGULAR((4,)),
         ],
         compiler_params=pltpu.CompilerParams(
-            collective_id=0, has_side_effects=True, vmem_limit_bytes=48 * 1024 * 1024
+            collective_id=0, has_side_effects=True, vmem_limit_bytes=62 * 1024 * 1024
         ),
     )(density, pattern)
 

time: 69.6 us -> 47.5 us (0.68)
  the two profiles are of different devices: /device:TPU:192 before, /device:TPU:704 now
where the time goes in v2:
time: 47.5 us; the launch traced here: 47.3 us
  Pallas kernels  45.5 us (96%)
  local copies, waits for them, and re-layouts  1.79 us (4%)
    pallas_call x1, Pallas kernels, on_device(): pl.pallas_call(kernel, out_shape=jax.ShapeDtypeStruct((1, ORB, BAND), F32...  45.5 us
    unnamed x1, local copies, waits for them, and re-layouts  1.79 us

profile of v2, /device:TPU:704, one launch (start us, length us, event | category | flops | bytes accessed | tf_op | source)
XLA Modules:
  0.0 47.3 jit_solution(6648196339501475940)
XLA Ops:
  0.0 45.5 %shard_map.28 = f32[1,64,1600]{2,1,0:T(8,128)} custom-call(f32[6,64,1600]{2,1,0:T(8,128)} %density.1, s32[6,25]{1,0:T(8,128)} %pattern_in.1), custom_call_target="tpu_custom_call" | custom-call | tf_op jit(solution)/shard_map/pallas_call | solution.py:438
  45.5 1.8 %copy.4 = f32[1,64,1600]{2,1,0:T(8,128)} copy(f32[1,64,1600]{2,1,0:T(8,128)} %shard_map.28) | data formatting | bytes 819200

commit v3 on v2

--- a/solution.py
+++ b/solution.py
@@ -9,6 +9,7 @@
 ORB = 64
 ROWS = 6
 CHIP = 2 * ROWS
+PIECES = 3 * ROWS
 FRAME = 3 * CHIP * ORB
 SIDE = CHIP * ORB
 HALFSIDE = ROWS * ORB
@@ -17,33 +18,55 @@
 TILE = 256
 DIAG = 12 * ORB
 F32 = jnp.float32
+VMEM_LIMIT = 63200 * 1024
 BF16 = jnp.bfloat16
 
 
-FIRST = (8, 10, 5, 2, 1, 0)
-SECOND = (6, 7, 9, 11, 4, 3)
+FIRST = (8, 10, 5, 2, 1)
+SECOND = (6, 3, 7, 9, 4, 11)
+COMMON = (6, 8, 7, 5, 9, 10, 11)
 LEFT_ORDER = (
-    (8, 10, 5, 2, 1, 6, 7, 9, 11, 4, 3, 0),
-    (8, 10, 5, 6, 7, 9, 11, 2, 4, 1, 3),
-    (6, 7, 9, 11, 8, 10, 5, 4, 3, 2),
-    (6, 7, 9, 11, 4, 3, 8, 10, 5),
-    (6, 7, 9, 11, 4, 8, 10, 5),
-    (6, 7, 9, 11, 8, 10, 5),
+    (8, 10, 6, 7, 9, 11, 5, 2, 3, 1, 4, 0),
+    (8, 10, 5, 2, 6, 3, 1, 7, 9, 4, 11),
+    (6, 3, 7, 9, 4, 11, 8, 10, 5, 2),
+    (6, 3, 7, 9, 4, 11, 8, 10, 5),
+    (4, *COMMON),
+    COMMON,
 )
 LEFT_NEXT = (
-    {1: FIRST},
-    {2: FIRST, 0: SECOND},
-    {3: FIRST + SECOND, 1: SECOND},
-    {4: FIRST + SECOND},
-    {5: FIRST + SECOND},
     {},
+    {2: (8, 10, 5, 2), 3: (8, 10, 5), 0: (*FIRST, 3, 4)},
+    {1: SECOND, 3: SECOND, 4: (4,), 0: (6, 7, 9, 11)},
+    {},
+    {},
+    {4: COMMON},
 )
-RIGHT_REACH = (9, 9, 9, 10, 11, 12)
-RIGHT_NEXT = ((1,), (2,), (), (), (3,), (4,))
+RIGHT_REACH = (7, 9, 9, 10, 12, 12)
+RIGHT_NEXT = ((), (0, 2), (), (), (3, 5), ())
 NEXT = (LEFT_NEXT, RIGHT_NEXT)
-ENTRY = ({5: 0, 0: 2}, {5: 0, 0: 5})
-EARLY_GIVER = (((1, 0), (1, 2), (2, 3), (3, 4), (4, 5)), ((0, 1), (1, 2)))
-NEAR_FIRST = (6, 0, 7, 8, 1, 9, 10, 11, 2, 3, 4, 5)
+ORDER = (
+    (6, 0, 7, 8, 1, 9, 10, 11, 2, 3, 4, 5),
+    (6, 0, 1, 7, 2, 8, 3, 9, 4, 10, 5, 11, 12, 13, 14, 15, 16, 17),
+)
+ENTRY = (
+    ((5, 1, FIRST), (5, 0, (0,)), (0, 2, SECOND), (0, 5, COMMON)),
+    ((5, 1, ORDER[1]), (0, 4, ORDER[1])),
+)
+EARLY_GIVER = (((1, 2), (1, 3), (1, 0), (2, 3), (2, 4)), ((1, 2), (4, 5)))
+EARLY_SLOT = (2, 3, 4, 5)
+SLOTS = 6
+
+
+def row_of(p):
+    return p % CHIP
+
+
+def core_of(p):
+    return row_of(p) // ROWS
+
+
+def cores_of(order):
+    return sorted({core_of(p) for p in order})
 
 
 def lanes(blocks):
@@ -68,7 +91,7 @@
     density, pattern_in, out,
     pattern, rows, big, small, wc_hi, wc_lo, big_hi, big_lo, small_hi, small_lo,
     left, middle, square, cube, maskrow,
-    pattern_sem, own_sem, pair_send, pair_recv, up_send, down_send, big_recv, fwd_send, fwd_recv, relay_a, relay_b, ready,
+    pattern_sem, own_sem, pair_send, pair_recv, up_send, down_send, big_recv, fwd_send, fwd_recv, relay_send, ready,
 ):
     wire = lax.axis_index("wire")
     length = lax.axis_size("wire")
@@ -121,22 +144,30 @@
         greet(source, me)
         greet(source + 1, me)
 
-    for end, target in ((first, down), (last, up)):
-        expected += counted(jnp.logical_not(end), 1)
-        expected += counted(jnp.logical_and(end, jnp.logical_and(ends, late)), 1)
-    for side, (end, target) in enumerate(((last, up), (first, down))):
-        for d, entry in ENTRY[side].items():
-            @when(end, early, m == d)
-            def _(target=target, entry=entry):
-                greet(target, entry)
+    expected += counted(jnp.logical_not(first), 1) + counted(jnp.logical_not(last), 1)
+    entries = [
+        (slot, kind, (last, first)[kind], (up, down)[kind], (seam_left, seam_right)[kind], *entry)
+        for slot, (kind, entry) in enumerate((k, e) for k in range(2) for e in ENTRY[k])
+    ]
+    for slot, kind, end, target, here, giver, taker, order in entries:
+        for core in cores_of(order):
+            gives = jnp.logical_and(jnp.logical_and(end, h == core), m == giver)
+            takes = jnp.logical_and(here, m == taker)
+            if slot in EARLY_SLOT:
+                expected += counted(jnp.logical_and(gives, late), 1)
+                expected += counted(jnp.logical_and(takes, late), 1)
+
+                @when(gives, early)
+                def _(target=target, taker=taker):
+                    greet(target, taker)
+            else:
+                expected += counted(gives, 1)
+
+            @when(takes, early if slot in EARLY_SLOT else True)
+            def _(giver=giver, core=core):
+                greet(source + core, giver)
 
     for kind, here in enumerate((seam_left, seam_right)):
-        for d, entry in ENTRY[kind].items():
-            @when(here, early, m == entry)
-            def _(d=d):
-                greet(source, d)
-                greet(source + 1, d)
-            expected += counted(jnp.logical_and(jnp.logical_and(here, late), m == entry), 2)
         for giver in range(ROWS):
             for taker in NEXT[kind][giver]:
                 asks = (giver, taker) in EARLY_GIVER[kind]
@@ -153,67 +184,80 @@
             ready.at[slot], inc=1, device_id={"wire": w, "depth": d}, device_id_type=MESH
         )
 
+    for slot, kind, end, target, here, giver, taker, order in entries:
+        for core in cores_of(order) if slot in EARLY_SLOT else ():
+            @when(here, late, m == taker)
+            def _(giver=giver, core=core, slot=slot):
+                is_ready(source + core, giver, slot)
+
     for kind, here in enumerate((seam_left, seam_right)):
-        for d, entry in ENTRY[kind].items():
-            @when(here, late, m == entry)
-            def _(d=d, kind=kind):
-                is_ready(source, d, kind)
-                is_ready(source + 1, d, kind)
         for giver in range(ROWS):
             for n, taker in enumerate(NEXT[kind][giver]):
                 if (giver, taker) in EARLY_GIVER[kind]:
                     @when(here, m == taker)
                     def _(giver=giver, n=n):
-                        is_ready(wire, giver, 2 + n)
-
-    def row_copy(s, t, width, target, depth, sem):
+                        is_ready(wire, giver, SLOTS + n)
+
+    def part(kind, p, reach):
+        t = row_of(p)
+        if kind == 0 or t >= ROWS:
+            return t, 0, lanes(reach - t)
+        near = lanes(ROWS - t)
+        return (t, 0, near) if p < CHIP else (t, near, lanes(reach - t) - near)
+
+    def row_copy(kind, p, reach, target, depth, second=0):
+        t, start, width = part(kind, p, reach)
+        sem = down_send.at[t % ROWS + p // CHIP * ROWS] if kind else up_send.at[t % ROWS + second * ROWS]
         return pltpu.make_async_remote_copy(
-            src_ref=density.at[s, :, pl.ds(DIAG, width)],
-            dst_ref=big.at[t, :, pl.ds(0, width)],
-            send_sem=sem.at[s], recv_sem=big_recv.at[t],
+            src_ref=density.at[t % ROWS, :, pl.ds(DIAG + start, width)],
+            dst_ref=big.at[t, :, pl.ds(start, width)],
+            send_sem=sem, recv_sem=big_recv.at[p],
             device_id={"wire": target, "depth": depth}, device_id_type=MESH,
         )
 
-    def send(act, core, order, target, depth, sem, reach):
-        for t in order:
-            if t // ROWS == core and t < reach:
-                act(row_copy(t % ROWS, t, lanes(reach - t), target, depth, sem))
+    def present(kind, p, reach):
+        return row_of(p) < reach and part(kind, p, reach)[2] > 0
+
+    def send(act, kind, core, order, target, depth, reach, second=0):
+        for p in order:
+            if core_of(p) == core and present(kind, p, reach):
+                act(row_copy(kind, p, reach, target, depth, second))
 
     def outgoing(act):
         for core in range(2):
+            @when(h == core, jnp.logical_not(first))
+            def _(core=core):
+                send(act, 1, core, ORDER[1][:CHIP], down, me, CHIP)
+
             @when(h == core, jnp.logical_not(last))
             def _(core=core):
-                send(act, core, NEAR_FIRST, up, me, up_send, CHIP)
+                send(act, 0, core, ORDER[0], up, me, CHIP)
 
             @when(h == core, jnp.logical_not(first))
             def _(core=core):
-                send(act, core, NEAR_FIRST, down, me, down_send, CHIP)
-
-    def crossing(act, whose, wait):
-        for core in range(2):
-            for d, entry in ENTRY[0].items():
-                @when(h == core, whose, last, m == d)
-                def _(core=core, d=d, entry=entry):
+                send(act, 1, core, ORDER[1][CHIP:], down, me, CHIP)
+
+    def crossing(act, whose, deferred, wait):
+        for slot, kind, end, target, here, giver, taker, order in entries:
+            if deferred and slot not in EARLY_SLOT:
+                continue
+            for core in cores_of(order):
+                @when(h == core, whose if slot in EARLY_SLOT else True, end, m == giver)
+                def _(core=core, slot=slot, kind=kind, target=target, taker=taker, order=order):
                     if wait:
-                        pl.semaphore_wait(ready.at[0], 1)
-                    send(act, core, FIRST if d else SECOND, up, entry, up_send, CHIP)
-
-            for d, entry in ENTRY[1].items():
-                @when(h == core, whose, first, m == d)
-                def _(core=core, d=d, entry=entry):
-                    if wait:
-                        pl.semaphore_wait(ready.at[1], 1)
-                    reach = RIGHT_REACH[2] if d else CHIP
-                    send(act, core, NEAR_FIRST, down, entry, down_send, reach)
-
-    def arriving(t, width):
-        return row_copy(t % ROWS, t, width, up, me, up_send)
-
-    def relay(t, width, depth, sem):
+                        pl.semaphore_wait(ready.at[slot], 1)
+                    reach = RIGHT_REACH[taker] if kind else CHIP
+                    send(act, kind, core, order, target, taker, reach, slot == 3)
+
+    def arriving(kind, p, reach):
+        return row_copy(kind, p, reach, up, me)
+
+    def relay(kind, p, reach, depth, n):
+        t, start, width = part(kind, p, reach)
         return pltpu.make_async_remote_copy(
-            src_ref=big.at[t, :, pl.ds(0, width)],
-            dst_ref=big.at[t, :, pl.ds(0, width)],
-            send_sem=sem.at[t], recv_sem=big_recv.at[t],
+            src_ref=big.at[t, :, pl.ds(start, width)],
+            dst_ref=big.at[t, :, pl.ds(start, width)],
+            send_sem=relay_send.at[n, p], recv_sem=big_recv.at[p],
             device_id={"wire": wire, "depth": depth}, device_id_type=MESH,
         )
 
@@ -226,54 +270,51 @@
             device_id={"wire": other}, device_id_type=MESH,
         )
 
-    def hand_on(t, core):
-        if t // ROWS == 1 - core:
-            forward(t % ROWS, core).start()
+    def hand_on(p, core):
+        if p < CHIP and core_of(p) == 1 - core:
+            forward(p % ROWS, core).start()
 
     def relays(kind, i):
         if kind == 0:
             for n, (target, which) in enumerate(LEFT_NEXT[i].items()):
-                sem = (relay_a, relay_b)[n]
-                for t in LEFT_ORDER[i]:
-                    if t in which and t in LEFT_ORDER[target]:
-                        yield t, relay(t, lanes(CHIP - t), target, sem)
-        for target in RIGHT_NEXT[i] if kind else ():
-            for t in NEAR_FIRST:
-                if t < RIGHT_REACH[target]:
-                    yield t, relay(t, lanes(RIGHT_REACH[target] - t), target, relay_a)
+                for p in LEFT_ORDER[i]:
+                    if p in which and p in LEFT_ORDER[target]:
+                        yield p, relay(0, p, CHIP, target, n)
+        for n, target in enumerate(RIGHT_NEXT[i] if kind else ()):
+            for p in ORDER[1]:
+                if present(1, p, RIGHT_REACH[target]):
+                    yield p, relay(1, p, RIGHT_REACH[target], target, n)
 
     def collect():
         for core in range(2):
             @when(h == core, jnp.logical_not(seam))
             def _(core=core):
-                for t in NEAR_FIRST:
-                    if t // ROWS == 1 - core:
-                        arriving(t, lanes(CHIP - t)).wait_recv()
-                        hand_on(t, core)
-                for t in NEAR_FIRST:
-                    if t // ROWS == core:
-                        arriving(t, lanes(CHIP - t)).wait_recv()
+                for near in (True, False):
+                    for p in ORDER[core]:
+                        if (p < CHIP and core_of(p) == 1 - core) == near:
+                            arriving(core, p, CHIP).wait_recv()
+                            hand_on(p, core)
         for i in range(ROWS):
             for kind, here in enumerate((seam_left, seam_right)):
                 @when(here, m == i)
                 def _(i=i, kind=kind):
-                    order = NEAR_FIRST if kind else LEFT_ORDER[i]
+                    order = ORDER[1] if kind else LEFT_ORDER[i]
                     reach = RIGHT_REACH[i] if kind else CHIP
                     onward = list(relays(kind, i))
                     for n, taker in enumerate(NEXT[kind][i]):
                         if (i, taker) in EARLY_GIVER[kind]:
-                            pl.semaphore_wait(ready.at[2 + n], 1)
-                    for t in order:
-                        if t < reach:
-                            arriving(t, lanes(reach - t)).wait_recv()
-                            for u, copy in onward:
-                                if u == t:
+                            pl.semaphore_wait(ready.at[SLOTS + n], 1)
+                    for p in order:
+                        if present(kind, p, reach):
+                            arriving(kind, p, reach).wait_recv()
+                            for q, copy in onward:
+                                if q == p:
                                     copy.start()
-                            hand_on(t, kind)
+                            hand_on(p, kind)
 
     def drain():
         outgoing(lambda copy: copy.wait_send())
-        crossing(lambda copy: copy.wait_send(), True, False)
+        crossing(lambda copy: copy.wait_send(), True, False, False)
         pair.wait_send()
         for core in range(2):
             @pl.when(h == core)
@@ -292,7 +333,7 @@
         send_sem=pair_send, recv_sem=pair_recv,
         device_id={"wire": other}, device_id_type=MESH,
     )
-    crossing(lambda copy: copy.start(), late, False)
+    crossing(lambda copy: copy.start(), late, False, False)
     outgoing(lambda copy: copy.start())
     pair.start()
 
@@ -393,7 +434,7 @@
     stack(middle, masked, mid)
     centre(middle, cube)
 
-    crossing(lambda copy: copy.start(), early, True)
+    crossing(lambda copy: copy.start(), early, True, True)
     collect()
 
     def build_triangle(source_ref, high_ref, low_ref, count):
@@ -456,11 +497,11 @@
             pltpu.VMEM((ORB, FRAME), F32),
             pltpu.VMEM((ORB, FRAME), F32),
             pltpu.VMEM((8, FRAME), F32),
-            dma, dma, dma, dma, dma((ROWS,)), dma((ROWS,)), dma((CHIP,)), dma((ROWS,)), dma((ROWS,)),
-            dma((CHIP,)), dma((CHIP,)), pltpu.SemaphoreType.REGULAR((4,)),
+            dma, dma, dma, dma, dma((CHIP,)), dma((CHIP,)), dma((PIECES,)), dma((ROWS,)), dma((ROWS,)),
+            dma((4, PIECES)), pltpu.SemaphoreType.REGULAR((SLOTS + 4,)),
         ],
         compiler_params=pltpu.CompilerParams(
-            collective_id=0, has_side_effects=True, vmem_limit_bytes=62 * 1024 * 1024
+            collective_id=0, has_side_effects=True, vmem_limit_bytes=VMEM_LIMIT
         ),
     )(density, pattern)
 

time: 47.5 us -> 42.7 us (0.90)
  the two profiles are of different devices: /device:TPU:704 before, /device:TPU:1 now
where the time goes in v3:
time: 42.7 us; the launch traced here: 42.6 us
  Pallas kernels  40.7 us (95%)
  local copies, waits for them, and re-layouts  1.79 us (4%)
    pallas_call x1, Pallas kernels, on_device(): pl.pallas_call(kernel, out_shape=jax.ShapeDtypeStruct((1, ORB, BAND), F32...  40.7 us
    unnamed x1, local copies, waits for them, and re-layouts  1.79 us

profile of v3, /device:TPU:1, one launch (start us, length us, event | category | flops | bytes accessed | tf_op | source)
XLA Modules:
  0.0 42.6 jit_solution(6642106873140551851)
XLA Ops:
  0.0 40.7 %shard_map.28 = f32[1,64,1600]{2,1,0:T(8,128)} custom-call(f32[6,64,1600]{2,1,0:T(8,128)} %density.1, s32[6,25]{1,0:T(8,128)} %pattern_in.1), custom_call_target="tpu_custom_call" | custom-call | tf_op jit(solution)/shard_map/pallas_call | solution.py:479
  40.8 1.8 %copy.4 = f32[1,64,1600]{2,1,0:T(8,128)} copy(f32[1,64,1600]{2,1,0:T(8,128)} %shard_map.28) | data formatting | bytes 819200

commit v4 on v3

--- a/solution.py
+++ b/solution.py
@@ -18,24 +18,24 @@
 TILE = 256
 DIAG = 12 * ORB
 F32 = jnp.float32
-VMEM_LIMIT = 63200 * 1024
+VMEM_LIMIT = 54000 * 1024
 BF16 = jnp.bfloat16
 
 
 FIRST = (8, 10, 5, 2, 1)
-SECOND = (6, 3, 7, 9, 4, 11)
+SECOND = (6, 7, 3, 9, 11, 4)
 COMMON = (6, 8, 7, 5, 9, 10, 11)
 LEFT_ORDER = (
-    (8, 10, 6, 7, 9, 11, 5, 2, 3, 1, 4, 0),
-    (8, 10, 5, 2, 6, 3, 1, 7, 9, 4, 11),
-    (6, 3, 7, 9, 4, 11, 8, 10, 5, 2),
-    (6, 3, 7, 9, 4, 11, 8, 10, 5),
+    (8, 10, 6, 7, 9, 11, 5, 2, 3, 4, 1, 0),
+    (8, 10, 5, 2, 6, 7, 3, 1, 9, 11, 4),
+    (6, 7, 3, 9, 11, 4, 8, 10, 5, 2),
+    (6, 7, 3, 9, 11, 4, 8, 10, 5),
     (4, *COMMON),
     COMMON,
 )
 LEFT_NEXT = (
     {},
-    {2: (8, 10, 5, 2), 3: (8, 10, 5), 0: (*FIRST, 3, 4)},
+    {2: (8, 10, 5, 2), 3: (8, 10, 5), 0: (8, 10, 5, 2, 3, 4)},
     {1: SECOND, 3: SECOND, 4: (4,), 0: (6, 7, 9, 11)},
     {},
     {},
@@ -49,7 +49,7 @@
     (6, 0, 1, 7, 2, 8, 3, 9, 4, 10, 5, 11, 12, 13, 14, 15, 16, 17),
 )
 ENTRY = (
-    ((5, 1, FIRST), (5, 0, (0,)), (0, 2, SECOND), (0, 5, COMMON)),
+    ((5, 1, FIRST), (5, 0, (1, 0)), (0, 2, SECOND), (0, 5, COMMON)),
     ((5, 1, ORDER[1]), (0, 4, ORDER[1])),
 )
 EARLY_GIVER = (((1, 2), (1, 3), (1, 0), (2, 3), (2, 4)), ((1, 2), (4, 5)))
@@ -247,7 +247,7 @@
                     if wait:
                         pl.semaphore_wait(ready.at[slot], 1)
                     reach = RIGHT_REACH[taker] if kind else CHIP
-                    send(act, kind, core, order, target, taker, reach, slot == 3)
+                    send(act, kind, core, order, target, taker, reach, slot in (1, 3))
 
     def arriving(kind, p, reach):
         return row_copy(kind, p, reach, up, me)

time: 42.7 us -> 40 us (0.937)
  Pallas kernels: 40.7 us -> 38.3 us
    pallas_call x1, Pallas kernels: 40.7 us -> 38.3 us  [on_device(): pl.pallas_call(kernel, out_shape=jax.ShapeDtypeStruct((1, ORB, BAND), F32...]
    unnamed x1 -> x3, local copies, waits for them, and re-layouts: 1.79 us -> 1.45 us
where the time goes in v4:
time: 40 us; the launch traced here: 39.8 us
  Pallas kernels  38.3 us (96%)
  local copies, waits for them, and re-layouts  1.45 us (4%)
    pallas_call x1, Pallas kernels, on_device(): pl.pallas_call(kernel, out_shape=jax.ShapeDtypeStruct((1, ORB, BAND), F32...  38.3 us
    unnamed x3, local copies, waits for them, and re-layouts  1.45 us

profile of v4, /device:TPU:1, one launch (start us, length us, event | category | flops | bytes accessed | tf_op | source)
XLA Modules:
  0.0 39.8 jit_solution(1790752125440293641)
XLA Ops:
  0.0 0.0 copy-start
  0.0 0.7 %copy-done = s32[6,25]{1,0:T(8,128)S(1)} copy-done((s32[6,25]{1,0:T(8,128)S(1)}, s32[6,25]{1,0:T(8,128)}, u32[]{:S(2)}) %copy-start) | copy-done | bytes 624
  0.7 38.3 %shard_map.28 = f32[1,64,1600]{2,1,0:T(8,128)S(1)} custom-call(f32[6,64,1600]{2,1,0:T(8,128)} %density.1, s32[6,25]{1,0:T(8,128)S(1)} %copy-done), custom_call_target="tpu_custom_call" | custom-call | tf_op jit(solution)/shard_map/pallas_call | solution.py:479
  39.0 0.8 %copy.4 = f32[1,64,1600]{2,1,0:T(8,128)} copy(f32[1,64,1600]{2,1,0:T(8,128)S(1)} %shard_map.28) | data formatting | bytes 819200
Async XLA Ops:
  0.0 0.7 %copy-start = (s32[6,25]{1,0:T(8,128)S(1)}, s32[6,25]{1,0:T(8,128)}, u32[]{:S(2)}) copy-start(s32[6,25]{1,0:T(8,128)} %pattern_in.1) | copy-start | bytes 1804

commit v5 on v4

--- a/solution.py
+++ b/solution.py
@@ -30,31 +30,33 @@
     (8, 10, 5, 2, 6, 7, 3, 1, 9, 11, 4),
     (6, 7, 3, 9, 11, 4, 8, 10, 5, 2),
     (6, 7, 3, 9, 11, 4, 8, 10, 5),
-    (4, *COMMON),
+    (*COMMON, 4),
     COMMON,
 )
 LEFT_NEXT = (
     {},
-    {2: (8, 10, 5, 2), 3: (8, 10, 5), 0: (8, 10, 5, 2, 3, 4)},
-    {1: SECOND, 3: SECOND, 4: (4,), 0: (6, 7, 9, 11)},
+    {2: (8, 10, 5, 2), 3: (8, 10, 5), 0: (8, 10, 5, 2, 6, 7, 9, 11)},
+    {1: SECOND, 3: SECOND, 4: (4,)},
     {},
+    {5: COMMON},
     {},
-    {4: COMMON},
 )
 RIGHT_REACH = (7, 9, 9, 10, 12, 12)
 RIGHT_NEXT = ((), (0, 2), (), (), (3, 5), ())
 NEXT = (LEFT_NEXT, RIGHT_NEXT)
+ASIDE = {1: (8, 10), 2: (6, 7, 9, 11)}
 ORDER = (
     (6, 0, 7, 8, 1, 9, 10, 11, 2, 3, 4, 5),
     (6, 0, 1, 7, 2, 8, 3, 9, 4, 10, 5, 11, 12, 13, 14, 15, 16, 17),
 )
 ENTRY = (
-    ((5, 1, FIRST), (5, 0, (1, 0)), (0, 2, SECOND), (0, 5, COMMON)),
+    ((5, 1, FIRST), (5, 0, (1, 3, 4, 0)), (0, 2, SECOND), (0, 4, COMMON)),
     ((5, 1, ORDER[1]), (0, 4, ORDER[1])),
 )
-EARLY_GIVER = (((1, 2), (1, 3), (1, 0), (2, 3), (2, 4)), ((1, 2), (4, 5)))
+EARLY_GIVER = (((1, 2), (1, 3), (1, 0), (2, 3), (2, 4), (4, 5)), ((1, 2), (4, 5)))
 EARLY_SLOT = (2, 3, 4, 5)
 SLOTS = 6
+LAST_SLOT = 1
 
 
 def row_of(p):
@@ -177,6 +179,15 @@
                 expected += counted(
                     jnp.logical_and(here, m == (taker if asks else giver)), 1
                 )
+    beside = jnp.logical_and(jnp.logical_and(h == 1, first), m == 0)
+    served = jnp.logical_and(seam_left, m == 0)
+    for giver in ASIDE:
+        expected += counted(jnp.logical_and(seam_left, m == giver), 1)
+
+        @pl.when(beside)
+        def _(giver=giver):
+            greet(other, giver)
+
     pl.semaphore_wait(barrier, expected)
 
     def is_ready(w, d, slot):
@@ -237,14 +248,16 @@
             def _(core=core):
                 send(act, 1, core, ORDER[1][CHIP:], down, me, CHIP)
 
-    def crossing(act, whose, deferred, wait):
+    def crossing(act, stage):
         for slot, kind, end, target, here, giver, taker, order in entries:
-            if deferred and slot not in EARLY_SLOT:
+            answered = slot in EARLY_SLOT and stage == 1
+            if stage < 2 and slot not in EARLY_SLOT and (slot == LAST_SLOT) != (stage == 1):
                 continue
+            whose = (late, early, True)[stage] if slot in EARLY_SLOT else True
             for core in cores_of(order):
-                @when(h == core, whose if slot in EARLY_SLOT else True, end, m == giver)
-                def _(core=core, slot=slot, kind=kind, target=target, taker=taker, order=order):
-                    if wait:
+                @when(h == core, whose, end, m == giver)
+                def _(core=core, slot=slot, kind=kind, target=target, taker=taker, order=order, answered=answered):
+                    if answered:
                         pl.semaphore_wait(ready.at[slot], 1)
                     reach = RIGHT_REACH[taker] if kind else CHIP
                     send(act, kind, core, order, target, taker, reach, slot in (1, 3))
@@ -270,12 +283,23 @@
             device_id={"wire": other}, device_id_type=MESH,
         )
 
+    def aside(t, n):
+        width = lanes(CHIP - t)
+        return pltpu.make_async_remote_copy(
+            src_ref=big.at[t, :, pl.ds(0, width)],
+            dst_ref=small.at[t - ROWS, :, pl.ds(0, width)],
+            send_sem=relay_send.at[n, t], recv_sem=fwd_recv.at[t - ROWS],
+            device_id={"wire": other, "depth": 0}, device_id_type=MESH,
+        )
+
     def hand_on(p, core):
         if p < CHIP and core_of(p) == 1 - core:
             forward(p % ROWS, core).start()
 
     def relays(kind, i):
         if kind == 0:
+            for p in ASIDE.get(i, ()):
+                yield p, aside(p, 4)
             for n, (target, which) in enumerate(LEFT_NEXT[i].items()):
                 for p in LEFT_ORDER[i]:
                     if p in which and p in LEFT_ORDER[target]:
@@ -310,14 +334,15 @@
                             for q, copy in onward:
                                 if q == p:
                                     copy.start()
-                            hand_on(p, kind)
+                            if kind or i:
+                                hand_on(p, kind)
 
     def drain():
         outgoing(lambda copy: copy.wait_send())
-        crossing(lambda copy: copy.wait_send(), True, False, False)
+        crossing(lambda copy: copy.wait_send(), 2)
         pair.wait_send()
         for core in range(2):
-            @pl.when(h == core)
+            @when(h == core, jnp.logical_not(served))
             def _(core=core):
                 for s in range(ROWS):
                     forward(s, core).wait_send()
@@ -333,7 +358,7 @@
         send_sem=pair_send, recv_sem=pair_recv,
         device_id={"wire": other}, device_id_type=MESH,
     )
-    crossing(lambda copy: copy.start(), late, False, False)
+    crossing(lambda copy: copy.start(), 0)
     outgoing(lambda copy: copy.start())
     pair.start()
 
@@ -434,7 +459,7 @@
     stack(middle, masked, mid)
     centre(middle, cube)
 
-    crossing(lambda copy: copy.start(), early, True, True)
+    crossing(lambda copy: copy.start(), 1)
     collect()
 
     def build_triangle(source_ref, high_ref, low_ref, count):
@@ -498,7 +523,7 @@
             pltpu.VMEM((ORB, FRAME), F32),
             pltpu.VMEM((8, FRAME), F32),
             dma, dma, dma, dma, dma((CHIP,)), dma((CHIP,)), dma((PIECES,)), dma((ROWS,)), dma((ROWS,)),
-            dma((4, PIECES)), pltpu.SemaphoreType.REGULAR((SLOTS + 4,)),
+            dma((5, PIECES)), pltpu.SemaphoreType.REGULAR((SLOTS + 4,)),
         ],
         compiler_params=pltpu.CompilerParams(
             collective_id=0, has_side_effects=True, vmem_limit_bytes=VMEM_LIMIT

time: 40 us -> 38.7 us (0.968)
  Pallas kernels: 38.3 us -> 37 us
    pallas_call x1, Pallas kernels: 38.3 us -> 37 us  [on_device(): pl.pallas_call(kernel, out_shape=jax.ShapeDtypeStruct((1, ORB, BAND), F32...]
where the time goes in v5:
time: 38.7 us; the launch traced here: 38.5 us
  Pallas kernels  37 us (96%)
  local copies, waits for them, and re-layouts  1.45 us (4%)
    pallas_call x1, Pallas kernels, on_device(): pl.pallas_call(kernel, out_shape=jax.ShapeDtypeStruct((1, ORB, BAND), F32...  37 us
    unnamed x3, local copies, waits for them, and re-layouts  1.45 us

profile of v5, /device:TPU:1, one launch (start us, length us, event | category | flops | bytes accessed | tf_op | source)
XLA Modules:
  0.0 38.5 jit_solution(6424468334311358113)
XLA Ops:
  0.0 0.0 copy-start
  0.0 0.7 %copy-done = s32[6,25]{1,0:T(8,128)S(1)} copy-done((s32[6,25]{1,0:T(8,128)S(1)}, s32[6,25]{1,0:T(8,128)}, u32[]{:S(2)}) %copy-start) | copy-done | bytes 624
  0.7 37.0 %shard_map.28 = f32[1,64,1600]{2,1,0:T(8,128)S(1)} custom-call(f32[6,64,1600]{2,1,0:T(8,128)} %density.1, s32[6,25]{1,0:T(8,128)S(1)} %copy-done), custom_call_target="tpu_custom_call" | custom-call | tf_op jit(solution)/shard_map/pallas_call | solution.py:504
  37.7 0.8 %copy.4 = f32[1,64,1600]{2,1,0:T(8,128)} copy(f32[1,64,1600]{2,1,0:T(8,128)S(1)} %shard_map.28) | data formatting | bytes 819200
Async XLA Ops:
  0.0 0.7 %copy-start = (s32[6,25]{1,0:T(8,128)S(1)}, s32[6,25]{1,0:T(8,128)}, u32[]{:S(2)}) copy-start(s32[6,25]{1,0:T(8,128)} %pattern_in.1) | copy-start | bytes 1804

commit v6 on v5

--- a/solution.py
+++ b/solution.py
@@ -36,7 +36,7 @@
 LEFT_NEXT = (
     {},
     {2: (8, 10, 5, 2), 3: (8, 10, 5), 0: (8, 10, 5, 2, 6, 7, 9, 11)},
-    {1: SECOND, 3: SECOND, 4: (4,)},
+    {1: (6, 7, 3, 9, 11), 3: SECOND, 4: (4,)},
     {},
     {5: COMMON},
     {},
@@ -50,12 +50,12 @@
     (6, 0, 1, 7, 2, 8, 3, 9, 4, 10, 5, 11, 12, 13, 14, 15, 16, 17),
 )
 ENTRY = (
-    ((5, 1, FIRST), (5, 0, (1, 3, 4, 0)), (0, 2, SECOND), (0, 4, COMMON)),
+    ((5, 1, FIRST), (5, 0, (1, 3, 4, 0)), (0, 2, SECOND), (0, 1, (4,)), (0, 4, COMMON)),
     ((5, 1, ORDER[1]), (0, 4, ORDER[1])),
 )
 EARLY_GIVER = (((1, 2), (1, 3), (1, 0), (2, 3), (2, 4), (4, 5)), ((1, 2), (4, 5)))
-EARLY_SLOT = (2, 3, 4, 5)
-SLOTS = 6
+EARLY_SLOT = (2, 3, 4, 5, 6)
+SLOTS = 7
 LAST_SLOT = 1
 
 
@@ -131,11 +131,12 @@
                 cond = jnp.logical_and(cond, c)
         return pl.when(cond)
 
+    greet(other, me)
+
     @pl.when(seam)
     def _():
         big[...] = jnp.zeros_like(big)
 
-    greet(other, me)
     expected = jnp.int32(1)
 
     def counted(cond, n):
@@ -260,7 +261,7 @@
                     if answered:
                         pl.semaphore_wait(ready.at[slot], 1)
                     reach = RIGHT_REACH[taker] if kind else CHIP
-                    send(act, kind, core, order, target, taker, reach, slot in (1, 3))
+                    send(act, kind, core, order, target, taker, reach, slot in (1, 3, 4))
 
     def arriving(kind, p, reach):
         return row_copy(kind, p, reach, up, me)

time: 38.7 us -> 38.6 us (level)
  no operation moved by 1% of the time
where the time goes in v6:
time: 38.6 us; the launch traced here: 38.4 us
  Pallas kernels  37 us (96%)
  local copies, waits for them, and re-layouts  1.45 us (4%)
    pallas_call x1, Pallas kernels, on_device(): pl.pallas_call(kernel, out_shape=jax.ShapeDtypeStruct((1, ORB, BAND), F32...  37 us
    unnamed x3, local copies, waits for them, and re-layouts  1.45 us

profile of v6, /device:TPU:1, one launch (start us, length us, event | category | flops | bytes accessed | tf_op | source)
XLA Modules:
  0.0 38.4 jit_solution(1385440476176186043)
XLA Ops:
  0.0 0.0 copy-start
  0.0 0.7 %copy-done = s32[6,25]{1,0:T(8,128)S(1)} copy-done((s32[6,25]{1,0:T(8,128)S(1)}, s32[6,25]{1,0:T(8,128)}, u32[]{:S(2)}) %copy-start) | copy-done | bytes 624
  0.7 37.0 %shard_map.28 = f32[1,64,1600]{2,1,0:T(8,128)S(1)} custom-call(f32[6,64,1600]{2,1,0:T(8,128)} %density.1, s32[6,25]{1,0:T(8,128)S(1)} %copy-done), custom_call_target="tpu_custom_call" | custom-call | tf_op jit(solution)/shard_map/pallas_call | solution.py:505
  37.7 0.8 %copy.4 = f32[1,64,1600]{2,1,0:T(8,128)} copy(f32[1,64,1600]{2,1,0:T(8,128)S(1)} %shard_map.28) | data formatting | bytes 819200
Async XLA Ops:
  0.0 0.7 %copy-start = (s32[6,25]{1,0:T(8,128)S(1)}, s32[6,25]{1,0:T(8,128)}, u32[]{:S(2)}) copy-start(s32[6,25]{1,0:T(8,128)} %pattern_in.1) | copy-start | bytes 1804
